TPU v7x, 32 devices: a whole 2x2x4 slice. The times are simulated.
32 devices in a mesh: fsdp: 32 (over z, y, x, core).
Axes of the slice: x: 2, y: 2, z: 4, core: 2. Of those that a mesh axis runs over, the one named last changes fastest.
Arguments:
- loop_state: bfloat16 [65536, 256], P('fsdp'), may hold values from -6 to 6
- embedding: bfloat16 [65536, 256], P('fsdp'), may hold values from -6 to 6
- output_grad: bfloat16 [65536, 256], P('fsdp'), may hold values from -6 to 6
- entry_weight: bfloat16 [256, 768], P('fsdp'), may hold values from -0.375 to 0.375
- exit_weight: bfloat16 [256, 256], P('fsdp'), may hold values from -1.5 to 1.5
- lead_gain: bfloat16 [256], P('fsdp'), may hold values from 0.25 to 1.75
- lead_shift: bfloat16 [256], P('fsdp'), may hold values from -3 to 3
- expand_weight: bfloat16 [256, 1024], P('fsdp'), may hold values from -0.375 to 0.375
- reduce_weight: bfloat16 [1024, 256], P('fsdp'), may hold values from -0.25 to 0.25
- middle_gain: bfloat16 [256], P('fsdp'), may hold values from 0.25 to 1.75
- middle_shift: bfloat16 [256], P('fsdp'), may hold values from -3 to 3
- expand_bias: bfloat16 [1024], P('fsdp'), may hold values from -3 to 3
- reduce_bias: bfloat16 [256], P('fsdp'), may hold values from -3 to 3
Outputs:
- final_state: bfloat16 [65536, 256], P('fsdp')
- state_grad: float32 [65536, 256], P('fsdp')
- embed_grad: float32 [65536, 256], P('fsdp')
- entry_grad: float32 [256, 768], P('fsdp')
- exit_grad: float32 [256, 256], P('fsdp')
- lead_gain_grad: float32 [256], P('fsdp')
- lead_shift_grad: float32 [256], P('fsdp')
- expand_grad: float32 [256, 1024], P('fsdp')
- reduce_grad: float32 [1024, 256], P('fsdp')
- middle_gain_grad: float32 [256], P('fsdp')
- middle_shift_grad: float32 [256], P('fsdp')
- expand_bias_grad: float32 [1024], P('fsdp')
- reduce_bias_grad: float32 [256], P('fsdp')
All inputs are finite; a program needn't handle non-finite values.
Results may differ from a plain program's by a relative error of at most 0.013.
Values may be sent and summed in bfloat16 or wider, within the bound.
A program may use at most 192 MiB of HBM per device.

v0:
```python
import functools
import math
from types import SimpleNamespace

import jax
import jax.numpy as jnp
from jax import lax
from jax.experimental import pallas as pl
from jax.experimental.pallas import tpu as pltpu
from jax.sharding import PartitionSpec as P

F32, BF16 = jnp.float32, jnp.bfloat16
LEN = 1024
LOOPS = 2
EPS = 1e-05
D = 256
FF = 1024
HD = 64
BLK = 256
LOG2E = 1.4426950408889634
LN2 = 0.6931471805599453
INV_SQRT_2PI = 1.0 / math.sqrt(2.0 * math.pi)
NEG = -1e30


def dot_nn(a, b):
    return lax.dot_general(a, b, (((1,), (0,)), ((), ())), preferred_element_type=F32)


def dot_nt(a, b):
    return lax.dot_general(a, b, (((1,), (1,)), ((), ())), preferred_element_type=F32)


def dot_tn(a, b):
    return lax.dot_general(a, b, (((0,), (0,)), ((), ())), preferred_element_type=F32)


def norm_parts(x):
    mean = jnp.mean(x, axis=-1, keepdims=True)
    center = x - mean
    var = jnp.mean(center * center, axis=-1, keepdims=True)
    rstd = lax.rsqrt(var + EPS)
    return center * rstd, rstd


def norm_pull(xhat, rstd, gain, dy):
    dn = dy * gain
    m1 = jnp.mean(dn, axis=-1, keepdims=True)
    m2 = jnp.mean(dn * xhat, axis=-1, keepdims=True)
    return rstd * (dn - m1 - xhat * m2)


def gelu_parts(x):
    cdf = 0.5 + 0.5 * lax.erf(x * math.sqrt(0.5))
    return cdf, jnp.exp2((-0.5 * LOG2E) * (x * x))


def lane_iota(rows):
    return lax.broadcasted_iota(jnp.int32, (rows, 128), 1)


def three_parts(x):
    hi = x.astype(BF16).astype(F32)
    r = x - hi
    mid = r.astype(BF16).astype(F32)
    return hi, mid, r - mid


def spread_parts(x, lane, spare):
    hi, mid, lo = three_parts(x)
    return jnp.where(lane == spare, hi, jnp.where(lane == spare + 1, mid, jnp.where(lane == spare + 2, lo, 0.0)))


def head_pairs(seqs):
    return [(pair, s) for pair in range(2) for s in range(seqs)]


def pair_slices(pair, s):
    seq = slice(s * LEN, (s + 1) * LEN)
    return seq, [slice(part * D + pair * 128, part * D + pair * 128 + 128) for part in range(3)]


def attn_forward(qkv, p, att, lx, vt, seqs, hook=None):
    nblk = LEN // BLK
    for b in range(2):
        vt[b, 0, HD:] = jnp.ones((HD, LEN), BF16)
        vt[b, 1, :HD] = jnp.ones((HD, LEN), BF16)
    low = lane_iota(BLK) < HD
    keep = lax.broadcasted_iota(jnp.int32, (BLK, BLK), 0) <= lax.broadcasted_iota(jnp.int32, (BLK, BLK), 1)
    row = lax.broadcasted_iota(jnp.int32, (8, BLK), 0)
    works = head_pairs(seqs)

    def scores(w, j, h):
        seq, (cq, ck, _) = pair_slices(*works[w])
        r0 = seq.start
        q = qkv[p, r0 + j * BLK:r0 + (j + 1) * BLK, cq]
        zero = jnp.zeros_like(q)
        q = jnp.where(low, q, zero) if h == 0 else jnp.where(low, zero, q)
        return dot_nt(qkv[p, r0:r0 + (j + 1) * BLK, ck], q)

    units = [(w, j, h) for w in range(len(works)) for j in range(nblk) for h in range(2)]
    st = None
    outs, pieces = [], []
    for u, (w, j, h) in enumerate(units):
        seq, (cq, _, cv) = pair_slices(*works[w])
        if j == 0 and h == 0:
            if hook is not None:
                hook(w)
            v = qkv[p, seq, cv].T
            vt[w % 2, 0, :HD] = v[:HD]
            vt[w % 2, 1, HD:] = v[HD:]
        if st is None:
            st = scores(w, j, h)
        later = scores(*units[u + 1]) if u + 1 < len(units) else None
        diag = jnp.where(keep, st[j * BLK:], NEG)
        st = jnp.concatenate([st[: j * BLK], diag], axis=0) if j else diag
        top = jnp.max(st, axis=0, keepdims=True)
        pr = jnp.exp2(st - top).astype(BF16)
        ox = dot_nn(vt[w % 2, h, :, : (j + 1) * BLK], pr)
        mine, den = (ox[:HD], ox[HD:]) if h == 0 else (ox[HD:], ox[:HD])
        outs.append(mine * (1.0 / den))
        hi, mid, lo = three_parts(-(top + jnp.log(den[:8]) * LOG2E))
        pieces.append(jnp.where(row == 0, hi, jnp.where(row == 1, mid, jnp.where(row == 2, lo, 0.0))))
        if h == 1:
            rows = slice(seq.start + j * BLK, seq.start + (j + 1) * BLK)
            att[p, rows, cq] = jnp.concatenate(outs, axis=0).T.astype(BF16)
            blank = jnp.zeros((HD - 8, BLK), F32)
            lx[p, rows, cq] = jnp.concatenate([pieces[1], blank, pieces[0], blank], axis=0).T.astype(BF16)
            outs, pieces = [], []
        st = later


def attn_backward(qkv, p, att, lx, datt, vx, kx, qx, dox, dkt, dvt, dq, seqs, hook):
    nblk = LEN // BLK
    low = lane_iota(LEN) < HD
    lane = lane_iota(LEN)
    keep = lax.broadcasted_iota(jnp.int32, (BLK, BLK), 1) <= lax.broadcasted_iota(jnp.int32, (BLK, BLK), 0)
    one = jnp.ones((LEN, 128), BF16)

    def work(pair, s):
        hook(pair, s)
        seq = pl.ds(pl.multiple_of(s * LEN, LEN), LEN)
        cq, ck, cv = (pl.ds(pl.multiple_of(part * D + pair * 128, 128), 128) for part in range(3))
        v = qkv[p, seq, cv]
        vx[0] = jnp.where(low, v, one)
        vx[1] = jnp.where(low, one, v)
        k = qkv[p, seq, ck]
        kx[0] = jnp.where(low, k, one)
        kx[1] = jnp.where(low, one, k)
        q = qkv[p, seq, cq]
        ls = lx[p, seq, cq]
        qx[0] = jnp.where(low, q, ls)
        qx[1] = jnp.where(low, ls, q)
        do = datt[seq, cq]
        dof = do.astype(F32)
        prod = dof * att[p, seq, cq].astype(F32)
        in0 = jnp.sum(jnp.where(low, prod, 0.0), axis=-1, keepdims=True)
        in1 = jnp.sum(jnp.where(low, 0.0, prod), axis=-1, keepdims=True)
        dox[0] = jnp.where(low, dof, spread_parts(jnp.broadcast_to(-in0, (LEN, 128)), lane, HD)).astype(BF16)
        dox[1] = jnp.where(low, spread_parts(jnp.broadcast_to(-in1, (LEN, 128)), lane, 0), dof).astype(BF16)
        qt = q.T
        dot = do.T

        def products(h, i):
            a = i * BLK
            return dot_nt(qx[h, a:], kx[h, a:a + BLK]), dot_nt(dox[h, a:], vx[h, a:a + BLK])

        units = [(h, i) for h in range(2) for i in range(nblk)]
        ready = products(*units[0])
        for u, (h, i) in enumerate(units):
            later = products(*units[u + 1]) if u + 1 < len(units) else None
            sc, dp = ready
            a = i * BLK
            pr = jnp.exp2(sc)
            diag = jnp.where(keep, pr[:BLK], 0.0)
            pr = jnp.concatenate([diag, pr[BLK:]], axis=0) if i < nblk - 1 else diag
            ds = (pr * dp).astype(BF16)
            prb = pr.astype(BF16)
            mine = slice(h * HD, h * HD + HD)
            dvt[mine, a:a + BLK] = dot_nn(dot[:, a:], prb)[mine]
            dkt[mine, a:a + BLK] = dot_nn(qt[:, a:], ds)[mine]
            part = dot_nn(ds, kx[h, a:a + BLK])
            if i == 0:
                dq[h] = part
            else:
                dq[h, a:] += part
            ready = later
        qkv[p, seq, cq] = (jnp.where(low, dq[0], dq[1]) * 0.125).astype(BF16)
        qkv[p, seq, ck] = (dkt[...].T * LN2).astype(BF16)
        qkv[p, seq, cv] = dvt[...].T.astype(BF16)

    def step(w, carry):
        work(w // seqs, w % seqs)
        return carry

    lax.fori_loop(0, 2 * seqs, step, 0)


def digit_groups(n):
    groups = [(1, 2)]
    stride = 2
    while stride < n:
        size = min(4, n // stride)
        groups.append((stride, size))
        stride *= size
    return groups[::-1]


class Links:
    def __init__(self, n):
        self.groups = digit_groups(n)
        self.me = lax.axis_index("fsdp")
        self.digits = [(self.me // stride) % size for stride, size in self.groups]
        self.sizes = tuple(size for _, size in self.groups)

    def digit(self, g, t):
        return (self.digits[g] + t) % self.sizes[g]

    def peer(self, g, t):
        return self.me + (self.digit(g, t) - self.digits[g]) * self.groups[g][0]

    def barrier(self):
        sem = pltpu.get_barrier_semaphore()
        count = 0
        for g, size in enumerate(self.sizes):
            for t in range(1, size):
                pl.semaphore_signal(sem, inc=1, device_id=(self.peer(g, t),), device_id_type=pl.DeviceIdType.MESH)
                count += 1
        return lambda: pl.semaphore_wait(sem, count)

    def copy(self, src, dst, sems, g, t):
        return pltpu.make_async_remote_copy(
            src_ref=src,
            dst_ref=dst,
            send_sem=sems.at[0, g, t - 1],
            recv_sem=sems.at[1, g, t - 1],
            device_id=(self.peer(g, t),),
            device_id_type=pl.DeviceIdType.MESH,
        )

    def held(self, buf, g, t=0):
        tail = [self.digit(g, t)] + self.digits[g + 1:]
        return buf.at[(slice(None),) * g + tuple(tail)]

    def gather_start(self, buf, sems, g):
        for t in range(1, self.sizes[g]):
            self.copy(self.held(buf, g), self.held(buf, g), sems, g, t).start()

    def gather_wait(self, buf, sems, g):
        for t in range(1, self.sizes[g]):
            self.copy(self.held(buf, g), self.held(buf, g, -t), sems, g, t).wait_recv()
        for t in range(1, self.sizes[g]):
            self.copy(self.held(buf, g), self.held(buf, g), sems, g, t).wait_send()

    def reduce_start(self, part, got, sems, g):
        for t in range(1, self.sizes[g]):
            src = part.at[(slice(None),) * g + (self.digit(g, t),)]
            self.copy(src, got.at[t - 1], sems, g, t).start()

    def reduce_wait(self, part, got, sems, g):
        for t in range(1, self.sizes[g]):
            src = part.at[(slice(None),) * g + (self.digit(g, t),)]
            self.copy(src, got.at[t - 1], sems, g, t).wait()
        total = part[(slice(None),) * g + (self.digits[g],)].astype(F32)
        for t in range(1, self.sizes[g]):
            total = total + got[t - 1].astype(F32)
        return total

    def sum_start(self, part, got, sems, g):
        for t in range(1, self.sizes[g]):
            self.copy(part.at[g], got.at[g, t - 1], sems, g, t).start()

    def sum_wait(self, part, got, sems, g):
        for t in range(1, self.sizes[g]):
            self.copy(part.at[g], got.at[g, t - 1], sems, g, t).wait()
        total = part[g]
        for t in range(1, self.sizes[g]):
            total = total + got[g, t - 1]
        part[g + 1] = total


class Reduction:
    def __init__(self, links, first, rest, sems):
        self.links, self.parts, self.gots, self.sems = links, [first] + rest[1::2], rest[0::2], sems

    def start(self, step):
        self.links.reduce_start(self.parts[step], self.gots[step], self.sems, len(self.links.sizes) - 1 - step)

    def take(self, step):
        return self.links.reduce_wait(self.parts[step], self.gots[step], self.sems, len(self.links.sizes) - 1 - step)

    def turn(self, step):
        total = self.take(step)
        self.parts[step + 1][...] = total.astype(BF16)
        self.start(step + 1)


def pair_rows(x, t):
    return jnp.concatenate([x[:, 256 * t : 256 * t + 128], x[:, 256 * t + 128 : 256 * t + 256]], axis=0)


ENTRY_ROWS = 64
FEED_ROWS = 144
PAIR_ROWS = 32
FEED_VECS = 16
LEAD_VECS = 8
CHUNK = 256


ROWS = 1024


def mega_kernel(*refs, names, n, tokens, comm):
    o = SimpleNamespace(**dict(zip(names, refs)))
    seqs = tokens // LEN
    chunks = [slice(c, c + CHUNK) for c in range(0, FF, CHUNK)]

    def pack_parameters():
        d = tuple(links.digits)
        x = o.entry_s[...].astype(F32)
        for t in range(3):
            o.buf1[d + (pl.ds(16 * t, 16),)] = pair_rows(x, t).astype(BF16)
        o.vec[...] = jnp.zeros_like(o.vec)
        for i, r in enumerate((o.lead_g, o.lead_s, o.mid_g, o.mid_s, o.red_b)):
            o.vec[i:i + 1, 0:8] = r[...].astype(F32).reshape(1, 8)
        o.vec[8:9, 0:32] = o.exp_b[...].astype(F32).reshape(1, 32)
        low = pltpu.roll(o.vec[0:8, :], (links.me * 8) % 128, 1)
        high = pltpu.roll(jnp.broadcast_to(o.vec[8:9, :], (8, 128)), (links.me * 32) % 128, 1)
        row = lax.broadcasted_iota(jnp.int32, (8, 128), 0)
        high = jnp.where(row == links.me // 4, high, 0.0)
        o.buf1[d + (pl.ds(48, 16),)] = jnp.concatenate([low, high], axis=0).astype(BF16)

    def pack_more_parameters():
        d = tuple(links.digits)
        o.buf2[d + (pl.ds(0, 16),)] = pair_rows(o.exit_s[...].astype(F32), 0).astype(BF16)
        x = o.expand_s[...].astype(F32)
        for t in range(4):
            o.buf2[d + (pl.ds(16 + 16 * t, 16),)] = pair_rows(x, t).astype(BF16)
        for c in range(2):
            o.buf2[d + (pl.ds(80 + 32 * c, 32),)] = o.reduce_s[:, 128 * c:128 * c + 128]

    def unpack(buf, at, count, dst):
        for t in range(count // 2):
            x = buf[:, :, :, at + 16 * t:at + 16 * t + 16, :].astype(F32).reshape(n, 16, 128)
            dst[:, 256 * t:256 * t + 128] = x[:, :8].reshape(8 * n, 128).astype(BF16)
            dst[:, 256 * t + 128:256 * t + 256] = x[:, 8:].reshape(8 * n, 128).astype(BF16)

    def unpack_first():
        unpack(o.buf1, 0, 6, o.entry_w)
        v = o.buf1[:, :, :, 48:64, :].astype(F32).reshape(n, 16, 128)
        first = jnp.sum(v[: n // 2], axis=0)
        second = jnp.sum(v[n // 2:], axis=0)
        o.vecs[0:5, 0:128] = first[0:5]
        o.vecs[0:5, 128:256] = second[0:5]
        both = (first + second)[8:16]
        for c in range(8):
            o.eb[0:1, 128 * c:128 * c + 128] = both[c:c + 1]

    def unpack_second():
        unpack(o.buf2, 0, 2, o.exit_w)
        unpack(o.buf2, 16, 8, o.expand_w)
        for c in range(2):
            x = o.buf2[:, :, :, 80 + 32 * c:112 + 32 * c, :]
            o.reduce_w[:, 128 * c:128 * c + 128] = x.reshape(32 * n, 128)

    def turn_weights():
        o.entry_t[...] = o.entry_w[...].T
        o.exit_t[...] = o.exit_w[...].T
        o.expand_t[...] = o.expand_w[...].T
        o.reduce_t[...] = o.reduce_w[...].T

    def chunk_rows(grad, c):
        return grad[:, 128 * c:128 * c + 128].reshape(n, 8, 128)

    def store_rows(part, at, top, bottom):
        x = jnp.concatenate([top, bottom], axis=1).astype(BF16)
        part[:, :, :, at:at + 16, :] = x.reshape(links.sizes + (16, 128))

    def halves(row):
        return [row[:, :128], row[:, 128:]]

    def vector_rows(part, rows, count):
        for i, r in enumerate(rows):
            part[0, i:i + 1, :] = r
        if len(rows) < count:
            part[0, len(rows):count, :] = jnp.zeros((count - len(rows), 128), F32)

    def own_eight(total, at):
        both = jnp.where(links.me >= n // 2, total[at + 1:at + 2], total[at:at + 1])
        both = pltpu.roll(jnp.broadcast_to(both, (8, 128)), (128 - (links.me * 8) % 128) % 128, 1)
        return both[0:1, 0:8].reshape(8)

    def feed_pack():
        store_rows(o.buf2, 0, chunk_rows(o.g_exit, 0), chunk_rows(o.g_exit, 1))
        for t in range(4):
            store_rows(o.buf2, 16 + 16 * t, chunk_rows(o.g_expand, 2 * t), chunk_rows(o.g_expand, 2 * t + 1))
        for c in range(2):
            x = o.g_reduce_t[128 * c:128 * c + 128, :].T.astype(BF16)
            o.buf2[:, :, :, 80 + 32 * c:112 + 32 * c, :] = x.reshape(links.sizes + (32, 128))
        rows = halves(o.g_small[2:3, :]) + halves(o.g_small[3:4, :]) + halves(o.g_small[5:6, :])
        rows += [o.g_exp_b[:, 128 * c:128 * c + 128] for c in range(8)]
        vector_rows(o.feed_vec, rows, FEED_VECS)

    def feed_end(total):
        for c in range(2):
            o.exit_o[:, 128 * c:128 * c + 128] = total[8 * c:8 * c + 8]
            o.reduce_o[:, 128 * c:128 * c + 128] = total[80 + 32 * c:112 + 32 * c]
        for c in range(8):
            o.expand_o[:, 128 * c:128 * c + 128] = total[16 + 8 * c:24 + 8 * c]

    def feed_vec_end():
        total = o.feed_vec[len(links.sizes)]
        o.mid_g_o[...] = own_eight(total, 0)
        o.mid_s_o[...] = own_eight(total, 2)
        o.red_b_o[...] = own_eight(total, 4)
        row = lax.broadcasted_iota(jnp.int32, (8, 128), 0)
        x = jnp.sum(jnp.where(row == links.me // 4, total[6:14], 0.0), axis=0, keepdims=True)
        x = pltpu.roll(jnp.broadcast_to(x, (8, 128)), (128 - (links.me * 32) % 128) % 128, 1)
        o.exp_b_o[...] = x[0:1, 0:32].reshape(32)

    def pair_grad(pair, n1):
        cols = [slice(part * D + pair * 128, part * D + pair * 128 + 128) for part in range(3)]
        q, k, v = ((o.g_entry[:, c] + dot_tn(n1, o.qkv[0, :, c])).reshape(n, 8, 128) for c in cols)
        store_rows(o.buf1, PAIR_ROWS * pair, q, k)
        store_rows(o.buf1, PAIR_ROWS * pair + 16, v, jnp.zeros_like(v))

    def pair_end(pair, total):
        for part in range(3):
            at = part * D + pair * 128
            o.entry_o[:, at:at + 128] = total[8 * part:8 * part + 8]

    def lead_vec_end():
        total = o.lead_vec[len(links.sizes)]
        o.lead_g_o[...] = own_eight(total, 0)
        o.lead_s_o[...] = own_eight(total, 2)

    every = slice(0, tokens)

    def first_mixed(rows=every):
        return o.state_in[rows].astype(F32) + o.embed_in[rows].astype(F32)

    def lead_normed(xhat):
        return (xhat * o.vecs[0:1, :] + o.vecs[1:2, :]).astype(BF16)

    def middle_normed(xhat):
        return (xhat * o.vecs[2:3, :] + o.vecs[3:4, :]).astype(BF16)

    def enter(p):
        x = o.grad[...] + o.embed_in[...].astype(F32)
        o.total[...] = x
        n1 = lead_normed(norm_parts(x)[0])
        for i in range(3):
            y = dot_nn(n1, o.entry_w[:, i * D:(i + 1) * D])
            o.qkv[p, :, i * D:(i + 1) * D] = (y * (LOG2E * 0.125) if i == 0 else y).astype(BF16)

    def forward_chunk(n2, c):
        hid = dot_nn(n2, o.expand_w[:, c]) + o.eb[:, c]
        cdf, e = gelu_parts(hid)
        return (hid * cdf).astype(BF16), cdf + hid * (e * INV_SQRT_2PI)

    def backward_chunk(d_out, n2, act, gp, c):
        reduce_g = dot_tn(d_out, act)
        dh = dot_nn(d_out, o.reduce_t[:, c]) * gp
        bias_g = jnp.sum(dh, axis=0, keepdims=True)
        dh = dh.astype(BF16)
        expand_g = dot_tn(n2, dh)
        o.g_reduce_t[:, c] += reduce_g
        o.g_exp_b[:, c] += bias_g
        o.g_expand[:, c] += expand_g
        return dot_nn(dh, o.expand_t[c, :])

    def clear():
        for r in (o.g_entry, o.g_exit, o.g_expand, o.g_reduce_t, o.g_small, o.g_exp_b):
            r[...] = jnp.zeros_like(r)

    def add_small(at, row):
        o.g_small[at:at + 1, :] += row

    def feed_finish(p, rows, g, dn, xhat, rstd):
        add_small(5, jnp.sum(g, axis=0, keepdims=True))
        add_small(2, jnp.sum(dn * xhat, axis=0, keepdims=True))
        add_small(3, jnp.sum(dn, axis=0, keepdims=True))
        dm = g + norm_pull(xhat, rstd, o.vecs[2:3, :], dn)
        o.grad[rows] = dm
        db = dm.astype(BF16)
        o.g_exit[...] += dot_tn(o.att[p, rows], db)
        o.grad_in[rows] = dot_nn(db, o.exit_t[...]).astype(BF16)

    def feed_first(rows):
        mid = o.total[rows] + dot_nn(o.att[0, rows], o.exit_w[...])
        o.middle[rows] = mid
        n2 = middle_normed(norm_parts(mid)[0])
        res = mid + o.vecs[4:5, :]
        for c in chunks:
            act, gp = forward_chunk(n2, c)
            o.active[rows, c] = act
            o.gelup[rows, c] = gp.astype(BF16)
            res = res + dot_nn(act, o.reduce_w[c, :])
        o.grad[rows] = res

    def feed_last(rows):
        mid = o.total[rows] + dot_nn(o.att[1, rows], o.exit_w[...])
        o.grad[rows] = mid
        n2 = middle_normed(norm_parts(mid)[0])
        res = mid + o.vecs[4:5, :]
        d_out = o.grad_in[rows]
        dn = None
        for c in chunks:
            act, gp = forward_chunk(n2, c)
            res = res + dot_nn(act, o.reduce_w[c, :])
            part = backward_chunk(d_out, n2, act, gp, c)
            dn = part if dn is None else dn + part
        o.final[rows] = res.astype(BF16)
        xhat, rstd = norm_parts(o.grad[rows])
        feed_finish(1, rows, o.grad_in[rows].astype(F32), dn, xhat, rstd)

    def feed_back(rows):
        n2 = middle_normed(norm_parts(o.middle[rows])[0])
        d_out = o.grad[rows].astype(BF16)
        dn = None
        for c in chunks:
            part = backward_chunk(d_out, n2, o.active[rows, c], o.gelup[rows, c].astype(F32), c)
            dn = part if dn is None else dn + part
        xhat, rstd = norm_parts(o.middle[rows])
        feed_finish(0, rows, o.grad[rows], dn, xhat, rstd)

    def by_rows(phase):
        def part(i, carry):
            phase(pl.ds(pl.multiple_of(i * ROWS, ROWS), ROWS))
            return carry
        lax.fori_loop(0, tokens // ROWS, part, 0)

    def add_entry(p, x):
        o.g_entry[...] += dot_tn(lead_normed(norm_parts(x)[0]), o.qkv[p])

    def leave(p):
        dn = dot_nn(o.qkv[p], o.entry_t[...])
        last = p == LOOPS - 1
        xhat, rstd = norm_parts(jnp.where(last, o.total[...], first_mixed()))
        add_small(0, jnp.sum(dn * xhat, axis=0, keepdims=True))
        add_small(1, jnp.sum(dn, axis=0, keepdims=True))
        g = o.grad[...] + norm_pull(xhat, rstd, o.vecs[0:1, :], dn)
        o.grad[...] = g
        o.total[...] = g + jnp.where(last, 0.0, o.total[...])

    def forward(p, hook=None):
        pl.run_scoped(lambda vt: attn_forward(o.qkv, p, o.att, o.lx, vt, seqs, hook), pltpu.VMEM((2, 2, 128, LEN), BF16))

    def backward(p, hook):
        head = [pltpu.VMEM((2, LEN, 128), BF16)] * 4 + [pltpu.VMEM((128, LEN), F32)] * 2 + [pltpu.VMEM((2, LEN, 128), F32)]
        pl.run_scoped(lambda *bufs: attn_backward(o.qkv, p, o.att, o.lx, o.grad_in, *bufs, seqs, hook), *head)

    def forward_passes(hook, ready):
        def one(p, carry):
            enter(p)
            forward(p, lambda w: hook(p, w))

            @pl.when(p == 0)
            def _():
                ready()
                by_rows(feed_first)

            return carry

        lax.fori_loop(0, LOOPS, one, 0)
        by_rows(feed_last)

    def backward_passes(hook, pair_done, ready):
        def one(i, carry):
            p = LOOPS - 1 - i
            backward(p, lambda pair, s: hook(p, pair, s))

            @pl.when(p == LOOPS - 1)
            def _():
                add_entry(LOOPS - 1, o.total[...])

            @pl.when(p == 0)
            def _():
                pair_done()

            leave(p)

            @pl.when(p == LOOPS - 1)
            def _():
                by_rows(feed_back)
                ready()

            return carry

        lax.fori_loop(0, LOOPS, one, 0)

    if not comm:
        for i, r in enumerate((o.lead_g, o.lead_s, o.mid_g, o.mid_s, o.red_b)):
            o.vecs[i:i + 1, :] = r[...].astype(F32)
        o.eb[...] = o.exp_b[...].astype(F32)
        o.grad_in[...] = o.grad_h[...]
        o.grad[...] = o.state_in[...].astype(F32)
        turn_weights()
        clear()
        forward_passes(lambda p, w: None, lambda: None)
        backward_passes(lambda p, pair, s: None, lambda: add_entry(0, first_mixed()), lambda: None)
        o.g_reduce[...] = o.g_reduce_t[...].T
        for i in range(4):
            o.g_small[8 + i:9 + i, :] = o.g_exp_b[:, i * D:(i + 1) * D]
        return

    links = Links(n)
    last = len(links.sizes) - 1
    arrived = links.barrier()
    loads = [
        pltpu.make_async_copy(src, dst, o.load_sem.at[i])
        for i, (src, dst) in enumerate(((o.state_h, o.state_in), (o.embed_h, o.embed_in), (o.grad_h, o.grad_in)))
    ]
    for load in loads:
        load.start()
    pack_parameters()
    arrived()
    links.gather_start(o.buf1, o.sem1, 0)
    pack_more_parameters()
    clear()
    links.gather_wait(o.buf1, o.sem1, 0)
    links.gather_start(o.buf1, o.sem1, 1)
    links.gather_start(o.buf2, o.sem2, 0)
    for load in loads:
        load.wait()
    o.grad[...] = o.state_in[...].astype(F32)
    links.gather_wait(o.buf1, o.sem1, 1)
    links.gather_start(o.buf1, o.sem1, 2)
    links.gather_wait(o.buf2, o.sem2, 0)
    links.gather_start(o.buf2, o.sem2, 1)
    links.gather_wait(o.buf1, o.sem1, 2)
    unpack_first()

    def gather_more(p, w):
        if w == seqs:
            @pl.when(p == 0)
            def _():
                links.gather_wait(o.buf2, o.sem2, 1)
                links.gather_start(o.buf2, o.sem2, 2)

    def gather_end():
        links.gather_wait(o.buf2, o.sem2, 2)
        unpack_second()
        turn_weights()

    forward_passes(gather_more, gather_end)
    feed = Reduction(links, o.buf2, [o.feed_got0, o.feed_part1, o.feed_got1, o.feed_part2, o.feed_got2], o.sem3)
    first = Reduction(links, o.buf1.at[:, :, :, pl.ds(0, PAIR_ROWS), :], [o.pair0_got0, o.pair0_part1, o.pair0_got1, o.pair0_part2, o.pair0_got2], o.sem4)
    second = Reduction(links, o.buf1.at[:, :, :, pl.ds(PAIR_ROWS, PAIR_ROWS), :], [o.pair1_got0, o.pair1_part1, o.pair1_got1, o.pair1_part2, o.pair1_got2], o.sem5)
    feed_vec = (o.feed_vec, o.feed_vec_got, o.sem6)
    lead_vec = (o.lead_vec, o.lead_vec_got, o.sem7)

    def reduce_begin():
        feed_pack()
        feed.start(0)
        links.sum_start(*feed_vec, 0)

    def reduce_more(p, pair, s):
        @pl.when((p == 0) & (pair == 0) & (s == 1))
        def _():
            feed.turn(0)
            links.sum_wait(*feed_vec, 0)
            links.sum_start(*feed_vec, 1)

        @pl.when((p == 0) & (pair == 1) & (s == 0))
        def _():
            o.att[1] = lead_normed(norm_parts(first_mixed())[0])
            pair_grad(0, o.att[1])
            first.start(0)

        @pl.when((p == 0) & (pair == 1) & (s == seqs - 1))
        def _():
            feed.turn(1)
            first.turn(0)
            links.sum_wait(*feed_vec, 1)
            links.sum_start(*feed_vec, 2)

    def reduce_last():
        pair_grad(1, o.att[1])
        second.start(0)
        first.turn(1)

    backward_passes(reduce_more, reduce_last, reduce_begin)
    vector_rows(o.lead_vec, halves(o.g_small[0:1, :]) + halves(o.g_small[1:2, :]), LEAD_VECS)
    links.sum_start(*lead_vec, 0)
    second.turn(0)
    feed_end(feed.take(2))
    links.sum_wait(*feed_vec, 2)
    feed_vec_end()
    links.sum_wait(*lead_vec, 0)
    links.sum_start(*lead_vec, 1)
    second.turn(1)
    pair_end(0, first.take(2))
    links.sum_wait(*lead_vec, 1)
    links.sum_start(*lead_vec, 2)
    pair_end(1, second.take(2))
    links.sum_wait(*lead_vec, 2)
    lead_vec_end()


VECTOR_INPUTS = ("lead_g", "lead_s", "mid_g", "mid_s", "red_b", "exp_b")


def mega(n, tokens, comm):
    T = tokens
    vmem = pltpu.VMEM
    outs = [("final", (T, D), BF16), ("grad", (T, D), F32), ("total", (T, D), F32)]
    scratch = [
        ("qkv", vmem((2, T, 3 * D), BF16)), ("att", vmem((2, T, D), BF16)), ("lx", vmem((2, T, D), BF16)),
        ("middle", vmem((T, D), F32)), ("active", vmem((T, FF), BF16)), ("gelup", vmem((T, FF), BF16)),
        ("entry_t", vmem((3 * D, D), BF16)), ("exit_t", vmem((D, D), BF16)), ("expand_t", vmem((FF, D), BF16)), ("reduce_t", vmem((D, FF), BF16)),
        ("vecs", vmem((8, D), F32)), ("eb", vmem((1, FF), F32)),
        ("g_reduce_t", vmem((D, FF), F32)), ("g_exp_b", vmem((1, FF), F32)),
    ]
    grads = [("g_entry", (D, 3 * D)), ("g_exit", (D, D)), ("g_expand", (D, FF)), ("g_small", (16, D))]
    weights = [("entry_w", (D, 3 * D)), ("exit_w", (D, D)), ("expand_w", (D, FF)), ("reduce_w", (FF, D))]
    in_vmem, in_hbm = pl.BlockSpec(memory_space=pltpu.VMEM), pl.BlockSpec(memory_space=pl.ANY)
    if comm:
        ins = ("state_h", "embed_h", "grad_h", "entry_s", "exit_s", "expand_s", "reduce_s") + VECTOR_INPUTS
        in_specs = [in_hbm] * 3 + [in_vmem] * 10
        r, rr = D // n, FF // n
        outs += [
            ("entry_o", (r, 3 * D), F32), ("exit_o", (r, D), F32), ("lead_g_o", (r,), F32), ("lead_s_o", (r,), F32),
            ("expand_o", (r, FF), F32), ("reduce_o", (rr, D), F32), ("mid_g_o", (r,), F32), ("mid_s_o", (r,), F32),
            ("exp_b_o", (rr,), F32), ("red_b_o", (r,), F32),
        ]
        scratch += [(name, vmem((T, D), BF16)) for name in ("state_in", "embed_in", "grad_in")]
        scratch += [(name, vmem(shape, F32)) for name, shape in grads] + [(name, vmem(shape, BF16)) for name, shape in weights]
        s = tuple(size for _, size in digit_groups(n))
        scratch += [("vec", vmem((16, 128), F32))]
        scratch += [("buf1", vmem(s + (ENTRY_ROWS, 128), BF16)), ("buf2", vmem(s + (FEED_ROWS, 128), BF16))]
        for name, rows in (("pair0", PAIR_ROWS), ("pair1", PAIR_ROWS), ("feed", FEED_ROWS)):
            for step, g in enumerate((2, 1, 0)):
                scratch.append((f"{name}_got{step}", vmem((s[g] - 1,) + s[:g] + (rows, 128), BF16)))
                if g < 2:
                    scratch.append((f"{name}_part{step}", vmem(s[: g + 1] + (rows, 128), BF16)))
        for name, rows in (("feed_vec", FEED_VECS), ("lead_vec", LEAD_VECS)):
            scratch += [(name, vmem((len(s) + 1, rows, 128), F32)), (f"{name}_got", vmem((len(s), 3, rows, 128), F32))]
        scratch += [(f"sem{i}", pltpu.SemaphoreType.DMA((2, 3, 3))) for i in range(1, 8)] + [("load_sem", pltpu.SemaphoreType.DMA((3,)))]
        out_shape = [vmem(shape, dtype) for _, shape, dtype in outs]
        params = dict(vmem_limit_bytes=58 * 1024 * 1024, collective_id=0, has_side_effects=True)
    else:
        ins = ("state_in", "embed_in", "grad_h") + tuple(name for name, _ in weights) + VECTOR_INPUTS
        in_specs = [in_vmem] * len(ins)
        outs += [(name, shape, F32) for name, shape in grads] + [("g_reduce", (FF, D), F32)]
        out_shape = [jax.ShapeDtypeStruct(shape, dtype) for _, shape, dtype in outs]
        scratch += [("grad_in", vmem((T, D), BF16))]
        params = dict(vmem_limit_bytes=63 * 1024 * 1024)
    names = ins + tuple(out[0] for out in outs) + tuple(name for name, _ in scratch)
    return pl.pallas_call(
        functools.partial(mega_kernel, names=names, n=n, tokens=T, comm=comm),
        in_specs=in_specs,
        out_specs=[in_vmem] * len(outs),
        out_shape=out_shape,
        scratch_shapes=[shape for _, shape in scratch],
        compiler_params=pltpu.CompilerParams(**params),
        name="block",
    )


def drain_kernel(*refs):
    count = len(refs) // 2
    sems = refs[-1]
    copies = [pltpu.make_async_copy(refs[i], refs[count + i], sems.at[i]) for i in range(count)]
    for copy in copies:
        copy.start()
    for copy in copies:
        copy.wait()


def drain(*arrays):
    count = len(arrays)
    return pl.pallas_call(
        drain_kernel,
        in_specs=[pl.BlockSpec(memory_space=pltpu.VMEM)] * count,
        out_specs=[pl.BlockSpec(memory_space=pl.ANY)] * count,
        out_shape=[jax.ShapeDtypeStruct(a.shape, a.dtype) for a in arrays],
        scratch_shapes=[pltpu.SemaphoreType.DMA((count,))],
        compiler_params=pltpu.CompilerParams(vmem_limit_bytes=1024 * 1024),
        name="drain",
    )(*arrays)


def on_device(loop_state, embedding, output_grad, entry_weight, exit_weight, lead_gain, lead_shift, expand_weight, reduce_weight, middle_gain, middle_shift, expand_bias, reduce_bias):
    n = lax.axis_size("fsdp")
    tokens = loop_state.shape[0]
    vectors = (lead_gain, lead_shift, middle_gain, middle_shift, reduce_bias, expand_bias)
    weights = (entry_weight, exit_weight, expand_weight, reduce_weight)
    if entry_weight.shape[0] == 8 and len(digit_groups(n)) == 3:
        return tuple(drain(*mega(n, tokens, True)(loop_state, embedding, output_grad, *weights, *vectors)))
    shards = weights + vectors
    packed = jnp.concatenate([a.reshape(-1) for a in shards])
    whole = lax.all_gather(packed, "fsdp", axis=0)
    full, at = [], 0
    for a in shards:
        whole_a = whole[:, at : at + a.size].reshape((n * a.shape[0],) + a.shape[1:])
        full.append(whole_a if a.ndim == 2 else whole_a.reshape(1, -1))
        at += a.size
    final, grad, total, g_entry, g_exit, g_expand, small, g_reduce = mega(n, tokens, False)(loop_state, embedding, output_grad, *full)
    terms = (g_entry, g_exit, small[0], small[1], g_expand, g_reduce, small[2], small[3], small[8:12].reshape(-1), small[5])
    sums = lax.psum_scatter(jnp.concatenate([a.reshape(n, -1) for a in terms], axis=1), "fsdp", scatter_dimension=0, tiled=True)[0]
    outs, at = [], 0
    for a in terms:
        size = a.size // n
        outs.append(sums[at : at + size].reshape((a.shape[0] // n,) + a.shape[1:]))
        at += size
    return (final, grad, total, *outs)


def solution(mesh):
    two, one = P("fsdp", None), P("fsdp")
    in_specs = (two, two, two, two, two, one, one, two, two, one, one, one, one)
    out_specs = (two, two, two, two, two, one, one, two, two, one, one, one, one)
    return jax.shard_map(on_device, mesh=mesh, in_specs=in_specs, out_specs=out_specs, check_vma=False)
```

profile of v0, /device:TPU:0, one launch (start us, length us, event | category | flops | bytes accessed | tf_op | source)
XLA Modules:
  0.0 108.8 jit_solution(9128003472064644603)
XLA Ops:
  0.6 105.5 %block.1 = (bf16[2048,256]{1,0:T(8,128)(2,1)S(1)}, f32[2048,256]{1,0:T(8,128)S(1)}, f32[2048,256]{1,0:T(8,128)S(1)}, f32[8,768]{1,0:T(8,128)S(1)}, f32[8,256]{1,...) custom-call(bf16[2048,256]{1,0:T(8,128)(2,1)} %refs_0_.1, ...), custom_call_target="tpu_custom_call" | custom-call | tf_op jit(solution)/shard_map/block/pallas_call | solution.py:790
  106.2 2.5 %drain.1 = (bf16[2048,256]{1,0:T(8,128)(2,1)}, f32[2048,256]{1,0:T(8,128)}, f32[2048,256]{1,0:T(8,128)}, f32[8,768]{1,0:T(8,128)}, f32[8,256]{1,0:T(8,128)}, /*i...) custom-call(bf16[2048,256]{1,0:T(8,128)(2,1)S(1)} %get-tuple-element, ...), custom_call_target="tpu_custom_call" | custom-call | tf_op jit(solution)/shard_map/drain/pallas_call | solution.py:773
where the time goes:
time: 109 us
  Pallas kernels  108 us (99%)
    pallas_call x1, Pallas kernels, on_device(): mega(n, tokens, True)  106 us
    pallas_call x1, Pallas kernels, drain(): pl.pallas_call(drain_kernel, in_specs=[pl.BlockSpec(memory_space=pltpu.VM...  2.5 us

commit v1 on v0

--- a/solution.py
+++ b/solution.py
@@ -395,7 +395,7 @@
         for t in range(4):
             store_rows(o.buf2, 16 + 16 * t, chunk_rows(o.g_expand, 2 * t), chunk_rows(o.g_expand, 2 * t + 1))
         for c in range(2):
-            x = o.g_reduce_t[128 * c:128 * c + 128, :].T.astype(BF16)
+            x = o.g_reduce_t[128 * c:128 * c + 128, :].astype(BF16).T
             o.buf2[:, :, :, 80 + 32 * c:112 + 32 * c, :] = x.reshape(links.sizes + (32, 128))
         rows = halves(o.g_small[2:3, :]) + halves(o.g_small[3:4, :]) + halves(o.g_small[5:6, :])
         rows += [o.g_exp_b[:, 128 * c:128 * c + 128] for c in range(8)]
@@ -420,7 +420,8 @@
 
     def pair_grad(pair, n1):
         cols = [slice(part * D + pair * 128, part * D + pair * 128 + 128) for part in range(3)]
-        q, k, v = ((o.g_entry[:, c] + dot_tn(n1, o.qkv[0, :, c])).reshape(n, 8, 128) for c in cols)
+        grad = dot_tn(n1, jnp.concatenate([o.qkv[0, :, c] for c in cols], axis=1))
+        q, k, v = ((o.g_entry[:, c] + grad[:, 128 * i:128 * i + 128]).reshape(n, 8, 128) for i, c in enumerate(cols))
         store_rows(o.buf1, PAIR_ROWS * pair, q, k)
         store_rows(o.buf1, PAIR_ROWS * pair + 16, v, jnp.zeros_like(v))
 
@@ -533,15 +534,17 @@
     def add_entry(p, x):
         o.g_entry[...] += dot_tn(lead_normed(norm_parts(x)[0]), o.qkv[p])
 
-    def leave(p):
+    def lead_sums(p, x):
         dn = dot_nn(o.qkv[p], o.entry_t[...])
-        last = p == LOOPS - 1
-        xhat, rstd = norm_parts(jnp.where(last, o.total[...], first_mixed()))
-        add_small(0, jnp.sum(dn * xhat, axis=0, keepdims=True))
+        add_small(0, jnp.sum(dn * norm_parts(x)[0], axis=0, keepdims=True))
         add_small(1, jnp.sum(dn, axis=0, keepdims=True))
+        return dn
+
+    def leave(dn, x, before):
+        xhat, rstd = norm_parts(x)
         g = o.grad[...] + norm_pull(xhat, rstd, o.vecs[0:1, :], dn)
         o.grad[...] = g
-        o.total[...] = g + jnp.where(last, 0.0, o.total[...])
+        o.total[...] = g if before is None else before + g
 
     def forward(p, hook=None):
         pl.run_scoped(lambda vt: attn_forward(o.qkv, p, o.att, o.lx, vt, seqs, hook), pltpu.VMEM((2, 2, 128, LEN), BF16))
@@ -565,7 +568,7 @@
         lax.fori_loop(0, LOOPS, one, 0)
         by_rows(feed_last)
 
-    def backward_passes(hook, pair_done, ready):
+    def backward_passes(hook, ready):
         def one(i, carry):
             p = LOOPS - 1 - i
             backward(p, lambda pair, s: hook(p, pair, s))
@@ -573,15 +576,7 @@
             @pl.when(p == LOOPS - 1)
             def _():
                 add_entry(LOOPS - 1, o.total[...])
-
-            @pl.when(p == 0)
-            def _():
-                pair_done()
-
-            leave(p)
-
-            @pl.when(p == LOOPS - 1)
-            def _():
+                leave(lead_sums(LOOPS - 1, o.total[...]), o.total[...], None)
                 by_rows(feed_back)
                 ready()
 
@@ -598,7 +593,9 @@
         turn_weights()
         clear()
         forward_passes(lambda p, w: None, lambda: None)
-        backward_passes(lambda p, pair, s: None, lambda: add_entry(0, first_mixed()), lambda: None)
+        backward_passes(lambda p, pair, s: None, lambda: None)
+        add_entry(0, first_mixed())
+        leave(lead_sums(0, first_mixed()), first_mixed(), o.total[...])
         o.g_reduce[...] = o.g_reduce_t[...].T
         for i in range(4):
             o.g_small[8 + i:9 + i, :] = o.g_exp_b[:, i * D:(i + 1) * D]
@@ -675,15 +672,15 @@
             links.sum_wait(*feed_vec, 1)
             links.sum_start(*feed_vec, 2)
 
-    def reduce_last():
-        pair_grad(1, o.att[1])
-        second.start(0)
-        first.turn(1)
-
-    backward_passes(reduce_more, reduce_last, reduce_begin)
+    backward_passes(reduce_more, reduce_begin)
+    pair_grad(1, o.att[1])
+    second.start(0)
+    dn = lead_sums(0, first_mixed())
     vector_rows(o.lead_vec, halves(o.g_small[0:1, :]) + halves(o.g_small[1:2, :]), LEAD_VECS)
     links.sum_start(*lead_vec, 0)
     second.turn(0)
+    first.turn(1)
+    leave(dn, first_mixed(), o.total[...])
     feed_end(feed.take(2))
     links.sum_wait(*feed_vec, 2)
     feed_vec_end()

time: 109 us -> 108 us (level)
    pallas_call x1, Pallas kernels: 106 us -> 104 us  [on_device(): mega(n, tokens, True)]
where the time goes in v1:
time: 108 us
  Pallas kernels  107 us (99%)
    pallas_call x1, Pallas kernels, on_device(): mega(n, tokens, True)  104 us
    pallas_call x1, Pallas kernels, drain(): pl.pallas_call(drain_kernel, in_specs=[pl.BlockSpec(memory_space=pltpu.VM...  2.5 us

profile of v1, /device:TPU:0, one launch (start us, length us, event | category | flops | bytes accessed | tf_op | source)
XLA Modules:
  0.0 107.7 jit_solution(5382108314093146670)
XLA Ops:
  0.6 104.4 %block.1 = (bf16[2048,256]{1,0:T(8,128)(2,1)S(1)}, f32[2048,256]{1,0:T(8,128)S(1)}, f32[2048,256]{1,0:T(8,128)S(1)}, f32[8,768]{1,0:T(8,128)S(1)}, f32[8,256]{1,...) custom-call(bf16[2048,256]{1,0:T(8,128)(2,1)} %refs_0_.1, ...), custom_call_target="tpu_custom_call" | custom-call | tf_op jit(solution)/shard_map/block/pallas_call | solution.py:787
  105.0 2.5 %drain.1 = (bf16[2048,256]{1,0:T(8,128)(2,1)}, f32[2048,256]{1,0:T(8,128)}, f32[2048,256]{1,0:T(8,128)}, f32[8,768]{1,0:T(8,128)}, f32[8,256]{1,0:T(8,128)}, /*i...) custom-call(bf16[2048,256]{1,0:T(8,128)(2,1)S(1)} %get-tuple-element, ...), custom_call_target="tpu_custom_call" | custom-call | tf_op jit(solution)/shard_map/drain/pallas_call | solution.py:770

commit v2 on v1

--- a/solution.py
+++ b/solution.py
@@ -99,7 +99,7 @@
         return dot_nt(qkv[p, r0:r0 + (j + 1) * BLK, ck], q)
 
     units = [(w, j, h) for w in range(len(works)) for j in range(nblk) for h in range(2)]
-    st = None
+    ready = []
     outs, pieces = [], []
     for u, (w, j, h) in enumerate(units):
         seq, (cq, _, cv) = pair_slices(*works[w])
@@ -109,9 +109,9 @@
             v = qkv[p, seq, cv].T
             vt[w % 2, 0, :HD] = v[:HD]
             vt[w % 2, 1, HD:] = v[HD:]
-        if st is None:
-            st = scores(w, j, h)
-        later = scores(*units[u + 1]) if u + 1 < len(units) else None
+        while len(ready) < 3 and u + len(ready) < len(units):
+            ready.append(scores(*units[u + len(ready)]))
+        st = ready.pop(0)
         diag = jnp.where(keep, st[j * BLK:], NEG)
         st = jnp.concatenate([st[: j * BLK], diag], axis=0) if j else diag
         top = jnp.max(st, axis=0, keepdims=True)
@@ -127,7 +127,6 @@
             blank = jnp.zeros((HD - 8, BLK), F32)
             lx[p, rows, cq] = jnp.concatenate([pieces[1], blank, pieces[0], blank], axis=0).T.astype(BF16)
             outs, pieces = [], []
-        st = later
 
 
 def attn_backward(qkv, p, att, lx, datt, vx, kx, qx, dox, dkt, dvt, dq, seqs, hook):
@@ -534,6 +533,18 @@
     def add_entry(p, x):
         o.g_entry[...] += dot_tn(lead_normed(norm_parts(x)[0]), o.qkv[p])
 
+    def leave_last(rows):
+        x = o.total[rows]
+        xhat, rstd = norm_parts(x)
+        dqkv = o.qkv[LOOPS - 1, rows]
+        o.g_entry[...] += dot_tn(lead_normed(xhat), dqkv)
+        dn = dot_nn(dqkv, o.entry_t[...])
+        add_small(0, jnp.sum(dn * xhat, axis=0, keepdims=True))
+        add_small(1, jnp.sum(dn, axis=0, keepdims=True))
+        g = o.grad[rows] + norm_pull(xhat, rstd, o.vecs[0:1, :], dn)
+        o.grad[rows] = g
+        o.total[rows] = g
+
     def lead_sums(p, x):
         dn = dot_nn(o.qkv[p], o.entry_t[...])
         add_small(0, jnp.sum(dn * norm_parts(x)[0], axis=0, keepdims=True))
@@ -575,8 +586,7 @@
 
             @pl.when(p == LOOPS - 1)
             def _():
-                add_entry(LOOPS - 1, o.total[...])
-                leave(lead_sums(LOOPS - 1, o.total[...]), o.total[...], None)
+                by_rows(leave_last)
                 by_rows(feed_back)
                 ready()
 

time: 108 us -> 106 us (0.981)
  Pallas kernels: 107 us -> 105 us
    pallas_call x1, Pallas kernels: 104 us -> 103 us  [on_device(): mega(n, tokens, True)]
where the time goes in v2:
time: 106 us
  Pallas kernels  105 us (99%)
    pallas_call x1, Pallas kernels, on_device(): mega(n, tokens, True)  103 us
    pallas_call x1, Pallas kernels, drain(): pl.pallas_call(drain_kernel, in_specs=[pl.BlockSpec(memory_space=pltpu.VM...  2.5 us

profile of v2, /device:TPU:0, one launch (start us, length us, event | category | flops | bytes accessed | tf_op | source)
XLA Modules:
  0.0 106.0 jit_solution(15381004206985340435)
XLA Ops:
  0.6 102.7 %block.1 = (bf16[2048,256]{1,0:T(8,128)(2,1)S(1)}, f32[2048,256]{1,0:T(8,128)S(1)}, f32[2048,256]{1,0:T(8,128)S(1)}, f32[8,768]{1,0:T(8,128)S(1)}, f32[8,256]{1,...) custom-call(bf16[2048,256]{1,0:T(8,128)(2,1)} %refs_0_.1, ...), custom_call_target="tpu_custom_call" | custom-call | tf_op jit(solution)/shard_map/block/pallas_call | solution.py:797
  103.3 2.5 %drain.1 = (bf16[2048,256]{1,0:T(8,128)(2,1)}, f32[2048,256]{1,0:T(8,128)}, f32[2048,256]{1,0:T(8,128)}, f32[8,768]{1,0:T(8,128)}, f32[8,256]{1,0:T(8,128)}, /*i...) custom-call(bf16[2048,256]{1,0:T(8,128)(2,1)S(1)} %get-tuple-element, ...), custom_call_target="tpu_custom_call" | custom-call | tf_op jit(solution)/shard_map/drain/pallas_call | solution.py:780
